TPU v7x, 512 devices: a whole 4x8x8 slice. The times are simulated.
512 devices in a mesh: comp: 64 (over x, z, core), lat: 8 (over y).
Axes of the slice: x: 4, y: 8, z: 8, core: 2. Of those that a mesh axis runs over, the one named last changes fastest.
Arguments:
- spectrum: bfloat16 [1152, 65536], P(None, ('lat', 'comp')), may hold values from 0.049804688 to 2
- sea_cells: int32 [8, 8192], P('lat'), may hold values from 0 to 8191, as said below
- sea_count: int32 [8], P('lat'), may hold values from 4096 to 8192, as said below
- refraction: float32 [8, 8192], P('lat'), may hold values from -0.45 to 0.45
- wind_speed: float32 [8, 8192], P('lat'), may hold values from 0.5 to 5
- growth: float32 [1152], replicated, may hold values from 0.02 to 0.2
- damping: float32 [1152], replicated, may hold values from 0.05 to 0.5
- courant: float32 [32], replicated, may hold values from 0.15 to 0.35
Outputs:
- propagated: float32 [1152, 128, 512], P('comp', 'lat')
Inputs may be any that keep to these rules, and one draw needn't show every extreme that they name: `sea_cells`: the 8192 entries of a tile are distinct cells of its 16 x 512 block; the first sea_count of them are its sea points in slot order. `sea_count`: one tile has exactly 8192 sea points.
All inputs are finite; a program needn't handle non-finite values.
Results may differ from a plain program's by a relative error of at most 0.006.
Values may be sent and summed in bfloat16 or wider, within the bound.
A program may use at most 64 MiB of HBM per device.

v0:
```python
import math

import jax
import jax.numpy as jnp
from jax import lax
from jax.sharding import PartitionSpec as P

NDIR = 36
ROWS = 16
LON = 512
PROP_STEPS = 2


TWO_PI = 2.0 * math.pi


def padded_2(block, sides, width):
    for axis, dim in sides:
        count = lax.axis_size(axis)
        forward = [(i, i + 1) for i in range(count - 1)]
        backward = [(target, source) for source, target in forward]
        low = lax.ppermute(
            lax.slice_in_dim(block, block.shape[dim] - width, None, axis=dim), axis, forward
        )
        high = lax.ppermute(lax.slice_in_dim(block, 0, width, axis=dim), axis, backward)
        block = jnp.concatenate([low, block, high], axis=dim)
    return block


def refract(energy, bend_rate):
    minus_dir = jnp.roll(energy, 1, axis=-2)
    plus_dir = jnp.roll(energy, -1, axis=-2)
    return (
        energy
        + jnp.maximum(bend_rate, 0.0) * (minus_dir - energy)
        + jnp.maximum(-bend_rate, 0.0) * (plus_dir - energy)
    )


def quickest_face(upwind, downwind, farther, courant_number):
    magnitude = jnp.abs(courant_number)
    return (
        0.5 * (upwind + downwind)
        - 0.5 * magnitude * (downwind - upwind)
        - (1.0 - courant_number * courant_number) / 6.0 * (downwind - 2.0 * upwind + farther)
    )


def advance(grid_field, sea_mask, speed_x, speed_y):
    height = grid_field.shape[1]
    interior = grid_field[:, 2 : height - 2]
    inner_mask = sea_mask[2 : height - 2]
    ahead_cell = jnp.roll(interior, -1, axis=2)
    behind = jnp.roll(interior, 1, axis=2)
    beyond = jnp.roll(interior, -2, axis=2)
    face_x = jnp.where(
        speed_x >= 0.0,
        quickest_face(interior, ahead_cell, behind, speed_x),
        quickest_face(ahead_cell, interior, beyond, speed_x),
    )
    open_x = inner_mask * jnp.roll(inner_mask, -1, axis=1)
    flux_x = speed_x * face_x * open_x
    change_x = flux_x - jnp.roll(flux_x, 1, axis=2)
    lower_row = grid_field[:, 1 : height - 2]
    upper_row = grid_field[:, 2 : height - 1]
    below_row = grid_field[:, 0 : height - 3]
    above_row = grid_field[:, 3:height]
    face_y = jnp.where(
        speed_y >= 0.0,
        quickest_face(lower_row, upper_row, below_row, speed_y),
        quickest_face(upper_row, lower_row, above_row, speed_y),
    )
    open_y = sea_mask[1 : height - 2] * sea_mask[2 : height - 1]
    flux_y = speed_y * face_y * open_y
    change_y = flux_y[:, 1:] - flux_y[:, :-1]
    return (interior - change_x - change_y) * inner_mask


def extend(grid_field, sea_mask, rim_width):
    stacked = jnp.concatenate([grid_field, sea_mask], axis=0)
    padded = padded_2(stacked.astype(jnp.bfloat16), (("lat", 1),), rim_width).astype(stacked.dtype)
    return (padded[:-1], padded[-1])


def place_on_grid(values, targets):
    dir_count = values.shape[0]
    stacked = jnp.concatenate([values, jnp.ones((1, values.shape[1]), jnp.bfloat16)], axis=0)
    column_ids = jnp.arange(LON, dtype=jnp.int32)

    def one_row(row_index):
        cells = row_index * LON + column_ids
        selector = (targets[:, None] == cells[None, :]).astype(jnp.bfloat16)
        return jnp.dot(stacked, selector, preferred_element_type=jnp.float32)

    rows_out = lax.map(one_row, jnp.arange(ROWS, dtype=jnp.int32))
    placed = jnp.transpose(rows_out, (1, 0, 2))
    return (placed[:dir_count], placed[dir_count:])


def body(spectrum, sea_cells, sea_count, refraction, wind_speed, growth, damping, courant):
    comp_devices = lax.axis_size("comp")
    comp_index = lax.axis_index("comp")
    comp_count = spectrum.shape[0]
    freq_count = comp_count // NDIR
    dir_count = NDIR // 2
    tile_slots = sea_cells.shape[1]
    slot_dev = tile_slots // comp_devices
    tile_cells = ROWS * LON
    bend_rate = lax.dynamic_slice_in_dim(refraction[0], comp_index * slot_dev, slot_dev)
    wind_here = lax.dynamic_slice_in_dim(wind_speed[0], comp_index * slot_dev, slot_dev)
    energy = spectrum.astype(jnp.float32).reshape(freq_count, NDIR, slot_dev)
    refracted = refract(energy, bend_rate).reshape(comp_count, slot_dev)
    mean_energy = jnp.sum(refracted, axis=0) / comp_count
    net_rate = (
        growth[:, None] * wind_here[None, :]
        - damping[:, None] * (mean_energy / (mean_energy + 1.0))[None, :]
    )
    sourced = (refracted * jnp.exp(net_rate)).astype(jnp.bfloat16)
    regrouped = lax.all_to_all(sourced, "comp", split_axis=0, concat_axis=1, tiled=True)
    sea_total = sea_count[0]
    live_slot = jnp.arange(tile_slots, dtype=jnp.int32) < sea_total
    targets = jnp.where(live_slot, sea_cells[0], tile_cells)
    grid_field, sea_mask = place_on_grid(regrouped, targets)
    freq_index = comp_index // 2
    group_speed = lax.dynamic_index_in_dim(courant, freq_index, 0, keepdims=False)
    dir_index = comp_index % 2 * dir_count + jnp.arange(dir_count, dtype=jnp.int32)
    angles = dir_index.astype(jnp.float32) * (TWO_PI / NDIR)
    speed_x = (group_speed * jnp.cos(angles))[:, None, None]
    speed_y = (group_speed * jnp.sin(angles))[:, None, None]
    for substep in range(PROP_STEPS):
        padded, padded_mask = extend(grid_field, sea_mask, 2)
        grid_field = advance(padded, padded_mask, speed_x, speed_y)
    return grid_field


def solution(mesh):
    return jax.shard_map(
        body,
        mesh=mesh,
        in_specs=(
            P(None, ("lat", "comp")),
            P("lat", None),
            P("lat"),
            P("lat", None),
            P("lat", None),
            P(),
            P(),
            P(),
        ),
        out_specs=P("comp", "lat", None),
        check_vma=False,
    )
```

profile of v0, /device:TPU:16, one launch (start us, length us, event | category | flops | bytes accessed | tf_op | source)
XLA Modules:
  0.0 140.9 jit_solution(3949217412647982231)
XLA Ops:
  3.7 13.8 %all-to-all-start = ((bf16[64,18,128]{2,1,0:T(8,128)(2,1)}), bf16[64,18,128]{2,1,0:T(8,128)(2,1)S(1)}, u32[]{:S(2)}, u32[]{:S(2)}) async-start(bf16[64,18,128]{2,1,0:T(8,128)(2,1)} %all_to_all.14), calls=%async_computation | async-start | bytes 786432 | tf_op jit(solution)/shard_map/all_to_all | solution.py:119
  19.5 12.6 %all-to-all-done = bf16[64,18,128]{2,1,0:T(8,128)(2,1)S(1)} async-done(((bf16[64,18,128]{2,1,0:T(8,128)(2,1)}), bf16[64,18,128]{2,1,0:T(8,128)(2,1)S(1)}, u32[]{:S(2)}, u32[]{:S(2)}) %all-to-all-start) | async-done | bytes 294944 | tf_op jit(solution)/shard_map/all_to_all | solution.py:119
  32.5 79.8 %while.11 = (s32[]{:T(128)}, bf16[16,19,512]{2,0,1:T(8,128)(2,1)S(1)}, s32[8192]{0:T(1024)S(1)}, s32[16]{0:T(128)S(1)}, bf16[19,8192]{1,0:T(8,128)(2,1)S(1)}, /*index=5*/s32[]{:T(128)}, s32[1]{0:T(128)}, s32[]{:T(128)}) while((s32[]{:T(128)}, bf16[16,19,512]{2,0,1:T(8,128)(2,1)S(1)}, s32[8192]{0:T(1024)S(1)}, s32[16]{0:T(128)S(1)}, ...), condition=%wide.region_2.3_spmd.clone, body=%wide.region_1.2_spmd.clone.sunk | while | flops 163578368 | bytes 445557 | solution.py:95
  33.8 2.6 %fusion.63 = bf16[1,19,512]{2,1,0:T(8,128)(2,1)S(1)} fusion(bf16[19,8192]{1,0:T(8,128)(2,1)S(1)} %get-tuple-element.147, s32[512]{0:T(512)S(1)} %iota_add_fusion.2, s32[8192]{0:T(1024)S(1)} %get-tuple-element.145), kind=kOutput, calls=%fused_computation.5.clone.1 | convolution fusion | flops 163577856 | bytes 365568 | tf_op jit(solution)/shard_map/while/body/eval_jaxpr/dot_general | solution.py:93
  38.7 2.6 %fusion.63 = bf16[1,19,512]{2,1,0:T(8,128)(2,1)S(1)} fusion(bf16[19,8192]{1,0:T(8,128)(2,1)S(1)} %get-tuple-element.147, s32[512]{0:T(512)S(1)} %iota_add_fusion.2, s32[8192]{0:T(1024)S(1)} %get-tuple-element.145), kind=kOutput, calls=%fused_computation.5.clone.1 | convolution fusion | flops 163577856 | bytes 365568 | tf_op jit(solution)/shard_map/while/body/eval_jaxpr/dot_general | solution.py:93
  43.7 2.6 %fusion.63 = bf16[1,19,512]{2,1,0:T(8,128)(2,1)S(1)} fusion(bf16[19,8192]{1,0:T(8,128)(2,1)S(1)} %get-tuple-element.147, s32[512]{0:T(512)S(1)} %iota_add_fusion.2, s32[8192]{0:T(1024)S(1)} %get-tuple-element.145), kind=kOutput, calls=%fused_computation.5.clone.1 | convolution fusion | flops 163577856 | bytes 365568 | tf_op jit(solution)/shard_map/while/body/eval_jaxpr/dot_general | solution.py:93
  48.7 2.6 %fusion.63 = bf16[1,19,512]{2,1,0:T(8,128)(2,1)S(1)} fusion(bf16[19,8192]{1,0:T(8,128)(2,1)S(1)} %get-tuple-element.147, s32[512]{0:T(512)S(1)} %iota_add_fusion.2, s32[8192]{0:T(1024)S(1)} %get-tuple-element.145), kind=kOutput, calls=%fused_computation.5.clone.1 | convolution fusion | flops 163577856 | bytes 365568 | tf_op jit(solution)/shard_map/while/body/eval_jaxpr/dot_general | solution.py:93
  53.7 2.6 %fusion.63 = bf16[1,19,512]{2,1,0:T(8,128)(2,1)S(1)} fusion(bf16[19,8192]{1,0:T(8,128)(2,1)S(1)} %get-tuple-element.147, s32[512]{0:T(512)S(1)} %iota_add_fusion.2, s32[8192]{0:T(1024)S(1)} %get-tuple-element.145), kind=kOutput, calls=%fused_computation.5.clone.1 | convolution fusion | flops 163577856 | bytes 365568 | tf_op jit(solution)/shard_map/while/body/eval_jaxpr/dot_general | solution.py:93
  58.7 2.6 %fusion.63 = bf16[1,19,512]{2,1,0:T(8,128)(2,1)S(1)} fusion(bf16[19,8192]{1,0:T(8,128)(2,1)S(1)} %get-tuple-element.147, s32[512]{0:T(512)S(1)} %iota_add_fusion.2, s32[8192]{0:T(1024)S(1)} %get-tuple-element.145), kind=kOutput, calls=%fused_computation.5.clone.1 | convolution fusion | flops 163577856 | bytes 365568 | tf_op jit(solution)/shard_map/while/body/eval_jaxpr/dot_general | solution.py:93
  63.7 2.6 %fusion.63 = bf16[1,19,512]{2,1,0:T(8,128)(2,1)S(1)} fusion(bf16[19,8192]{1,0:T(8,128)(2,1)S(1)} %get-tuple-element.147, s32[512]{0:T(512)S(1)} %iota_add_fusion.2, s32[8192]{0:T(1024)S(1)} %get-tuple-element.145), kind=kOutput, calls=%fused_computation.5.clone.1 | convolution fusion | flops 163577856 | bytes 365568 | tf_op jit(solution)/shard_map/while/body/eval_jaxpr/dot_general | solution.py:93
  68.7 2.6 %fusion.63 = bf16[1,19,512]{2,1,0:T(8,128)(2,1)S(1)} fusion(bf16[19,8192]{1,0:T(8,128)(2,1)S(1)} %get-tuple-element.147, s32[512]{0:T(512)S(1)} %iota_add_fusion.2, s32[8192]{0:T(1024)S(1)} %get-tuple-element.145), kind=kOutput, calls=%fused_computation.5.clone.1 | convolution fusion | flops 163577856 | bytes 365568 | tf_op jit(solution)/shard_map/while/body/eval_jaxpr/dot_general | solution.py:93
  73.6 2.6 %fusion.63 = bf16[1,19,512]{2,1,0:T(8,128)(2,1)S(1)} fusion(bf16[19,8192]{1,0:T(8,128)(2,1)S(1)} %get-tuple-element.147, s32[512]{0:T(512)S(1)} %iota_add_fusion.2, s32[8192]{0:T(1024)S(1)} %get-tuple-element.145), kind=kOutput, calls=%fused_computation.5.clone.1 | convolution fusion | flops 163577856 | bytes 365568 | tf_op jit(solution)/shard_map/while/body/eval_jaxpr/dot_general | solution.py:93
  78.6 2.6 %fusion.63 = bf16[1,19,512]{2,1,0:T(8,128)(2,1)S(1)} fusion(bf16[19,8192]{1,0:T(8,128)(2,1)S(1)} %get-tuple-element.147, s32[512]{0:T(512)S(1)} %iota_add_fusion.2, s32[8192]{0:T(1024)S(1)} %get-tuple-element.145), kind=kOutput, calls=%fused_computation.5.clone.1 | convolution fusion | flops 163577856 | bytes 365568 | tf_op jit(solution)/shard_map/while/body/eval_jaxpr/dot_general | solution.py:93
  83.6 2.6 %fusion.63 = bf16[1,19,512]{2,1,0:T(8,128)(2,1)S(1)} fusion(bf16[19,8192]{1,0:T(8,128)(2,1)S(1)} %get-tuple-element.147, s32[512]{0:T(512)S(1)} %iota_add_fusion.2, s32[8192]{0:T(1024)S(1)} %get-tuple-element.145), kind=kOutput, calls=%fused_computation.5.clone.1 | convolution fusion | flops 163577856 | bytes 365568 | tf_op jit(solution)/shard_map/while/body/eval_jaxpr/dot_general | solution.py:93
  88.6 2.6 %fusion.63 = bf16[1,19,512]{2,1,0:T(8,128)(2,1)S(1)} fusion(bf16[19,8192]{1,0:T(8,128)(2,1)S(1)} %get-tuple-element.147, s32[512]{0:T(512)S(1)} %iota_add_fusion.2, s32[8192]{0:T(1024)S(1)} %get-tuple-element.145), kind=kOutput, calls=%fused_computation.5.clone.1 | convolution fusion | flops 163577856 | bytes 365568 | tf_op jit(solution)/shard_map/while/body/eval_jaxpr/dot_general | solution.py:93
  93.6 2.6 %fusion.63 = bf16[1,19,512]{2,1,0:T(8,128)(2,1)S(1)} fusion(bf16[19,8192]{1,0:T(8,128)(2,1)S(1)} %get-tuple-element.147, s32[512]{0:T(512)S(1)} %iota_add_fusion.2, s32[8192]{0:T(1024)S(1)} %get-tuple-element.145), kind=kOutput, calls=%fused_computation.5.clone.1 | convolution fusion | flops 163577856 | bytes 365568 | tf_op jit(solution)/shard_map/while/body/eval_jaxpr/dot_general | solution.py:93
  98.6 2.6 %fusion.63 = bf16[1,19,512]{2,1,0:T(8,128)(2,1)S(1)} fusion(bf16[19,8192]{1,0:T(8,128)(2,1)S(1)} %get-tuple-element.147, s32[512]{0:T(512)S(1)} %iota_add_fusion.2, s32[8192]{0:T(1024)S(1)} %get-tuple-element.145), kind=kOutput, calls=%fused_computation.5.clone.1 | convolution fusion | flops 163577856 | bytes 365568 | tf_op jit(solution)/shard_map/while/body/eval_jaxpr/dot_general | solution.py:93
  103.5 2.6 %fusion.63 = bf16[1,19,512]{2,1,0:T(8,128)(2,1)S(1)} fusion(bf16[19,8192]{1,0:T(8,128)(2,1)S(1)} %get-tuple-element.147, s32[512]{0:T(512)S(1)} %iota_add_fusion.2, s32[8192]{0:T(1024)S(1)} %get-tuple-element.145), kind=kOutput, calls=%fused_computation.5.clone.1 | convolution fusion | flops 163577856 | bytes 365568 | tf_op jit(solution)/shard_map/while/body/eval_jaxpr/dot_general | solution.py:93
  108.5 2.6 %fusion.63 = bf16[1,19,512]{2,1,0:T(8,128)(2,1)S(1)} fusion(bf16[19,8192]{1,0:T(8,128)(2,1)S(1)} %get-tuple-element.147, s32[512]{0:T(512)S(1)} %iota_add_fusion.2, s32[8192]{0:T(1024)S(1)} %get-tuple-element.145), kind=kOutput, calls=%fused_computation.5.clone.1 | convolution fusion | flops 163577856 | bytes 365568 | tf_op jit(solution)/shard_map/while/body/eval_jaxpr/dot_general | solution.py:93
  112.3 3.5 %collective-permute-start = (bf16[19,2,512]{2,1,0:T(2,128)(2,1)S(1)}, bf16[19,2,512]{2,1,0:T(2,128)(2,1)S(1)}, u32[]{:S(2)}, u32[]{:S(2)}) collective-permute-start(bf16[19,2,512]{2,1,0:T(2,128)(2,1)S(1)} %get-tuple-element.83), channel_id=1, source_target_pairs={{0,1},{1,2},{2,3},{3,4},{4,5},{5,6},{6,7},{8,9},{9,10},{10,11},{11... | collective-permute-start | bytes 116744 | tf_op jit(solution)/shard_map/ppermute | solution.py:22
  115.8 2.4 %collective-permute-start.1 = (bf16[19,2,512]{2,1,0:T(2,128)(2,1)S(1)}, bf16[19,2,512]{2,1,0:T(2,128)(2,1)S(1)}, u32[]{:S(2)}, u32[]{:S(2)}) collective-permute-start(bf16[19,2,512]{2,1,0:T(2,128)(2,1)S(1)} %get-tuple-element.84), channel_id=1, source_target_pairs={{1,0},{2,1},{3,2},{4,3},{5,4},{6,5},{7,6},{9,8},{10,9},{11,10},{12... | collective-permute-start | bytes 116744 | tf_op jit(solution)/shard_map/ppermute | solution.py:25
  118.2 4.3 %collective-permute-done.1 = bf16[19,2,512]{2,1,0:T(2,128)(2,1)S(1)} collective-permute-done((bf16[19,2,512]{2,1,0:T(2,128)(2,1)S(1)}, bf16[19,2,512]{2,1,0:T(2,128)(2,1)S(1)}, u32[]{:S(2)}, u32[]{:S(2)}) %collective-permute-start.1) | collective-permute-done | bytes 38944 | tf_op jit(solution)/shard_map/ppermute | solution.py:25
  125.8 5.1 %collective-permute-start.2 = (bf16[19,2,512]{2,1,0:T(2,128)(2,1)S(1)}, bf16[19,2,512]{2,1,0:T(2,128)(2,1)S(1)}, u32[]{:S(2)}, u32[]{:S(2)}) collective-permute-start(bf16[19,2,512]{2,1,0:T(2,128)(2,1)S(1)} %get-tuple-element.80), channel_id=1, source_target_pairs={{0,1},{1,2},{2,3},{3,4},{4,5},{5,6},{6,7},{8,9},{9,10},{10,11},{11... | collective-permute-start | bytes 116744 | tf_op jit(solution)/shard_map/ppermute | solution.py:22
  133.1 3.8 %collective-permute-done.3 = bf16[19,2,512]{2,1,0:T(2,128)(2,1)S(1)} collective-permute-done((bf16[19,2,512]{2,1,0:T(2,128)(2,1)S(1)}, bf16[19,2,512]{2,1,0:T(2,128)(2,1)S(1)}, u32[]{:S(2)}, u32[]{:S(2)}) %collective-permute-start.3) | collective-permute-done | bytes 38944 | tf_op jit(solution)/shard_map/ppermute | solution.py:25
  (129 shorter events, 41.2 us)
Async XLA Ops:
  1.3 1.0 copy-start
  1.4 1.1 copy-start.2
  1.4 1.1 copy-start.3
  2.9 15.3 %copy-start.4 = (f32[32]{0:T(128)S(1)}, f32[32]{0:T(128)}, u32[]{:S(2)}) copy-start(f32[32]{0:T(128)} %param.17) | copy-start | bytes 388
  2.9 16.5 %copy-start.1 = (s32[1,8192]{1,0:T(1,128)S(1)}, s32[1,8192]{1,0:T(1,128)}, u32[]{:S(2)}) copy-start(s32[1,8192]{1,0:T(1,128)} %param.11) | copy-start | bytes 98308
  3.7 28.3 %all-to-all-start = ((bf16[64,18,128]{2,1,0:T(8,128)(2,1)}), bf16[64,18,128]{2,1,0:T(8,128)(2,1)S(1)}, u32[]{:S(2)}, u32[]{:S(2)}) async-start(bf16[64,18,128]{2,1,0:T(8,128)(2,1)} %all_to_all.14), calls=%async_computation | async-start | bytes 786432 | tf_op jit(solution)/shard_map/all_to_all | solution.py:119
  112.3 5.9 %collective-permute-start = (bf16[19,2,512]{2,1,0:T(2,128)(2,1)S(1)}, bf16[19,2,512]{2,1,0:T(2,128)(2,1)S(1)}, u32[]{:S(2)}, u32[]{:S(2)}) collective-permute-start(bf16[19,2,512]{2,1,0:T(2,128)(2,1)S(1)} %get-tuple-element.83), channel_id=1, source_target_pairs={{0,1},{1,2},{2,3},{3,4},{4,5},{5,6},{6,7},{8,9},{9,10},{10,11},{11... | collective-permute-start | bytes 116744 | tf_op jit(solution)/shard_map/ppermute | solution.py:22
  115.8 6.6 %collective-permute-start.1 = (bf16[19,2,512]{2,1,0:T(2,128)(2,1)S(1)}, bf16[19,2,512]{2,1,0:T(2,128)(2,1)S(1)}, u32[]{:S(2)}, u32[]{:S(2)}) collective-permute-start(bf16[19,2,512]{2,1,0:T(2,128)(2,1)S(1)} %get-tuple-element.84), channel_id=1, source_target_pairs={{1,0},{2,1},{3,2},{4,3},{5,4},{6,5},{7,6},{9,8},{10,9},{11,10},{12... | collective-permute-start | bytes 116744 | tf_op jit(solution)/shard_map/ppermute | solution.py:25
  125.8 7.3 %collective-permute-start.2 = (bf16[19,2,512]{2,1,0:T(2,128)(2,1)S(1)}, bf16[19,2,512]{2,1,0:T(2,128)(2,1)S(1)}, u32[]{:S(2)}, u32[]{:S(2)}) collective-permute-start(bf16[19,2,512]{2,1,0:T(2,128)(2,1)S(1)} %get-tuple-element.80), channel_id=1, source_target_pairs={{0,1},{1,2},{2,3},{3,4},{4,5},{5,6},{6,7},{8,9},{9,10},{10,11},{11... | collective-permute-start | bytes 116744 | tf_op jit(solution)/shard_map/ppermute | solution.py:22
  130.9 5.9 %collective-permute-start.3 = (bf16[19,2,512]{2,1,0:T(2,128)(2,1)S(1)}, bf16[19,2,512]{2,1,0:T(2,128)(2,1)S(1)}, u32[]{:S(2)}, u32[]{:S(2)}) collective-permute-start(bf16[19,2,512]{2,1,0:T(2,128)(2,1)S(1)} %get-tuple-element.81), channel_id=1, source_target_pairs={{1,0},{2,1},{3,2},{4,3},{5,4},{6,5},{7,6},{9,8},{10,9},{11,10},{12... | collective-permute-start | bytes 116744 | tf_op jit(solution)/shard_map/ppermute | solution.py:25
where the time goes:
time: 141 us
  matrix products  42.2 us (30%)
  local copies, waits for them, and re-layouts  31.4 us (22%)
  starting transfers between devices  26.9 us (19%)
  waiting for transfers between devices  20.6 us (15%)
  loops' own time  11 us (8%)
  other arithmetic  7.62 us (5%)
    dot_general x16, matrix products, one_row(): return jnp.dot(stacked, selector, preferred_element_type=jnp.float32)  42.2 us
    dynamic_update_slice x32, local copies, waits for them, and re-layouts, place_on_grid(): rows_out = lax.map(one_row, jnp.arange(ROWS, dtype=jnp.int32))  17.1 us
    all_to_all x1, starting transfers between devices, body(): lax.all_to_all(sourced, 'comp', split_axis=0, concat_axis=1, tiled=True)  13.8 us
    all_to_all x1, waiting for transfers between devices, body(): lax.all_to_all(sourced, 'comp', split_axis=0, concat_axis=1, tiled=True)  12.6 us
    another operation x1, loops' own time, place_on_grid(): rows_out = lax.map(one_row, jnp.arange(ROWS, dtype=jnp.int32))  11 us
    dynamic_slice x16, local copies, waits for them, and re-layouts, place_on_grid(): rows_out = lax.map(one_row, jnp.arange(ROWS, dtype=jnp.int32))  9.38 us
    ppermute x2, starting transfers between devices, padded_2(): lax.ppermute(lax.slice_in_dim(block, block.shape[dim] - width, None, axis...  8.62 us
    ppermute x2, waiting for transfers between devices, padded_2(): lax.ppermute(lax.slice_in_dim(block, 0, width, axis=dim), axis, backward)  8.01 us
  transfers between devices with their start and end apart: 5, of which 3 were waited for; matrix products, arithmetic and copies ran while one was open for 1% of the time, Pallas kernels for 0%

commit v1 on v0

v1 whole, which is shorter than its diff:
```python
import math

import jax
import jax.numpy as jnp
import numpy as np
from jax import lax
from jax.experimental import pallas as pl
from jax.experimental.pallas import tpu as pltpu
from jax.sharding import PartitionSpec as P

MESH = pl.DeviceIdType.MESH
NDIR = 36
NCOMP = 1152
ROWS = 16
LON = 512
TILES = 8
SLOTS = 8192
PEERS = 64
NX, NZ, NCORE = 4, 8, 2
GROUP = NX * NCORE
BLOCK = 128
MINE = NCOMP // PEERS
MAIN = 16
EXT = ROWS + 8
CHUNK = 4 * NDIR

f32 = jnp.float32
bf16 = jnp.bfloat16


def direction_table():
    angles = np.arange(NDIR, dtype=np.float32) * np.float32(2.0 * math.pi / NDIR)
    pick = list(range(MAIN)) + [MAIN, MAIN + 1] * 4
    table = np.zeros((2, 2, 24, 128), np.float32)
    for half in range(2):
        rows = angles[half * MINE + np.array(pick)]
        table[half, 0] = np.cos(rows)[:, None]
        table[half, 1] = np.sin(rows)[:, None]
    return table


def face_weights(speed):
    size = jnp.abs(speed)
    third = (1.0 - speed * speed) / 6.0
    near = (0.5 + 0.5 * size + 2.0 * third) * speed
    far = (0.5 - 0.5 * size - third) * speed
    edge = -third * speed
    ahead = speed >= 0.0
    zero = jnp.zeros_like(speed)
    return (
        jnp.where(ahead, edge, zero),
        jnp.where(ahead, near, far),
        jnp.where(ahead, far, near),
        jnp.where(ahead, zero, edge),
    )


def kernel(
    spec_hbm, cells_hbm, count_hbm, refr_hbm, wind_hbm, growth_hbm, damp_hbm, cour_hbm, table_hbm, out_hbm,
    spec_v, cells_v, count_s, refr_v, wind_v, growth_v, damp_v, cour_s, table_v,
    growth_b, damp_b, bent, send, recv, cols, rowid, mask_bf, mask_in,
    mask_x, open_x, open_y, dense_m, dense_x, dense_y,
    field, mid, tail, tail_d, tail_mid, edge_out, edge_in, out_v,
    in_sem, send_sem, recv_sem, own_sem, mask_send, mask_recv, edge_send, edge_recv, out_sem,
):
    me = lax.axis_index("comp")
    lat = lax.axis_index("lat")
    mx, mz, mc = me // (NZ * NCORE), lax.rem(me, NZ * NCORE) // NCORE, lax.rem(me, NCORE)
    mq = mx * NCORE + mc
    upper, lower = lax.rem(lat + 1, TILES), lax.rem(lat + TILES - 1, TILES)

    barrier = pltpu.get_barrier_semaphore()

    def greet(i, carry):
        other = lax.rem(me + i, PEERS)
        pl.semaphore_signal(barrier, inc=1, device_id={"comp": other}, device_id_type=MESH)
        return carry

    lax.fori_loop(1, PEERS, greet, 0)
    for other in (upper, lower):
        pl.semaphore_signal(barrier, inc=1, device_id={"lat": other}, device_id_type=MESH)

    my_slots = pl.ds(pl.multiple_of(me * BLOCK, BLOCK), BLOCK)
    loads = [
        (spec_hbm, spec_v),
        (cells_hbm, cells_v),
        (count_hbm, count_s),
        (refr_hbm.at[:, my_slots], refr_v),
        (wind_hbm.at[:, my_slots], wind_v),
        (growth_hbm, growth_v),
        (damp_hbm, damp_v),
        (cour_hbm, cour_s),
        (table_hbm.at[lax.rem(me, 2)], table_v),
    ]
    copies = [pltpu.make_async_copy(src, dst, in_sem.at[i]) for i, (src, dst) in enumerate(loads)]
    for copy in copies:
        copy.start()
    for copy in copies:
        copy.wait()

    for j in range(NCOMP // 128):
        part = pl.ds(j * 128, 128)
        growth_b[part, :] = jnp.broadcast_to(growth_v[part].reshape(1, 128), (128, 128)).T
        damp_b[part, :] = jnp.broadcast_to(damp_v[part].reshape(1, 128), (128, 128)).T

    bend = refr_v[...]
    bend_up = jnp.broadcast_to(jnp.maximum(bend, 0.0), (CHUNK, BLOCK))
    bend_down = jnp.broadcast_to(jnp.maximum(-bend, 0.0), (CHUNK, BLOCK))
    dir_of = lax.rem(lax.broadcasted_iota(jnp.int32, (CHUNK, BLOCK), 0), NDIR)

    def refract(g, total):
        part = pl.ds(pl.multiple_of(g * CHUNK, CHUNK), CHUNK)
        energy = spec_v[part, :].astype(f32)
        before = jnp.where(dir_of == 0, pltpu.roll(energy, CHUNK - NDIR + 1, 0), pltpu.roll(energy, 1, 0))
        after = jnp.where(dir_of == NDIR - 1, pltpu.roll(energy, NDIR - 1, 0), pltpu.roll(energy, CHUNK - 1, 0))
        moved = energy + bend_up * (before - energy) + bend_down * (after - energy)
        bent[part, :] = moved
        return total + jnp.sum(moved.reshape(CHUNK // 8, 8, BLOCK), axis=0)

    total = lax.fori_loop(0, NCOMP // CHUNK, refract, jnp.zeros((8, BLOCK), f32))
    mean = jnp.sum(total, axis=0, keepdims=True) / NCOMP
    loss = jnp.broadcast_to(mean / (mean + 1.0), (CHUNK, BLOCK))
    wind = jnp.broadcast_to(wind_v[...], (CHUNK, BLOCK))
    send_rows = send.reshape(NCOMP, BLOCK)

    def source(g, carry):
        part = pl.ds(pl.multiple_of(g * CHUNK, CHUNK), CHUNK)
        rate = growth_b[part, :] * wind - damp_b[part, :] * loss
        send_rows[part, :] = (bent[part, :] * jnp.exp(rate)).astype(bf16)
        return carry

    lax.fori_loop(0, NCOMP // CHUNK, source, 0)

    pl.semaphore_wait(barrier, PEERS - 1 + 2)

    def z_of(k):
        steps = NZ // 2 - (k + 1) // 2
        return lax.rem(mz + jnp.where(lax.rem(k, 2) == 1, steps, NZ - steps), NZ)

    def give(k, j):
        q = lax.rem(mq + j, GROUP)
        other = (q // NCORE) * (NZ * NCORE) + z_of(k) * NCORE + lax.rem(q, NCORE)
        pltpu.make_async_remote_copy(
            src_ref=send.at[other],
            dst_ref=recv.at[mz * GROUP + mq],
            send_sem=send_sem,
            recv_sem=recv_sem.at[mz],
            device_id={"comp": other},
            device_id_type=MESH,
        ).start()

    def give_group(k, carry):
        lax.fori_loop(0, GROUP, lambda j, c: (give(k, j), c)[1], 0)
        return carry

    lax.fori_loop(0, NZ - 1, give_group, 0)
    lax.fori_loop(1, GROUP, lambda j, c: (give(NZ - 1, j), c)[1], 0)
    own = pltpu.make_async_copy(send.at[me], recv.at[mz * GROUP + mq], own_sem)
    own.start()

    live_count = count_s[0]
    lane = lax.broadcasted_iota(jnp.int32, (1, BLOCK), 1)
    col_of = lax.broadcasted_iota(jnp.int16, (LON, BLOCK), 0)
    row_of = lax.broadcasted_iota(jnp.int16, (ROWS, GROUP * BLOCK), 0)

    def factors(z, total):
        for q in range(GROUP):
            first = ((q // NCORE) * (NZ * NCORE) + z * NCORE + q % NCORE) * BLOCK
            cell = cells_v[:, pl.ds(pl.multiple_of(first, BLOCK), BLOCK)]
            col = jnp.broadcast_to(lax.bitwise_and(cell, LON - 1), (LON, BLOCK)).astype(jnp.int16)
            cols[z, :, q * BLOCK : (q + 1) * BLOCK] = jnp.where(col_of == col, bf16(1), bf16(0))
            row = jnp.where(lane + first < live_count, lax.shift_right_logical(cell, 9), ROWS)
            rowid[z, :, q * BLOCK : (q + 1) * BLOCK] = jnp.broadcast_to(row, (ROWS, BLOCK)).astype(jnp.int16)
        hot = jnp.where(rowid[z] == row_of, bf16(1), bf16(0))
        return total + lax.dot_general(hot, cols[z], (((1,), (1,)), ((), ())), preferred_element_type=f32)

    mask = lax.fori_loop(0, NZ, factors, jnp.zeros((ROWS, LON), f32))
    mask_bf[...] = mask.astype(bf16)
    mask_copies = []
    for i, other in enumerate((upper, lower)):
        copy = pltpu.make_async_remote_copy(
            src_ref=mask_bf,
            dst_ref=mask_in.at[i],
            send_sem=mask_send.at[i],
            recv_sem=mask_recv.at[i],
            device_id={"lat": other},
            device_id_type=MESH,
        )
        copy.start()
        mask_copies.append(copy)

    field[...] = jnp.zeros_like(field)
    tail[...] = jnp.zeros_like(tail)
    speed = cour_s[me // 2]
    wx = face_weights(speed * table_v[0])
    wy = face_weights(speed * table_v[1])

    def wide(w):
        return jnp.concatenate([w[:MAIN]] * (LON // 128), axis=1)

    main_x, main_y = [wide(w) for w in wx], [wide(w) for w in wy]
    tail_x, tail_y = [w[MAIN:][None] for w in wx], [w[MAIN:][None] for w in wy]

    for copy in mask_copies:
        copy.wait()
    has_lower = jnp.where(lat > 0, 1.0, 0.0)
    has_upper = jnp.where(lat < TILES - 1, 1.0, 0.0)
    below = mask_in[0].astype(f32)[ROWS - 4 :] * has_lower
    above = mask_in[1].astype(f32)[:4] * has_upper
    full = jnp.concatenate([below, mask, above], axis=0)
    mask_x[...] = full
    open_x[...] = full * pltpu.roll(full, LON - 1, 1)
    open_y[...] = full * pltpu.roll(full, EXT - 1, 0)
    for wide_m, dense in ((mask_x, dense_m), (open_x, dense_x), (open_y, dense_y)):
        for t in range(EXT // 8):
            for b in range(LON // 128):
                piece = wide_m[t * 8 : (t + 1) * 8, b * 128 : (b + 1) * 128]
                for p in range(2):
                    dense[pl.ds(t * 64 + b * 2 + p, 8, stride=8), :] = piece

    recv_rows = recv.reshape(PEERS * MINE, BLOCK)

    def place(z):
        ids = rowid[z]
        main, rest = [], []
        for q in range(GROUP):
            first = (z * GROUP + q) * MINE
            main.append(recv_rows[pl.ds(first, MAIN), :])
            rest.append(recv_rows[pl.ds(first + MAIN, 2), :])
        main = jnp.concatenate(main, axis=1)
        rest = jnp.concatenate(rest, axis=1)
        parts = [jnp.where(ids == r, main, bf16(0)) for r in range(ROWS)]
        for p in range(2):
            line = jnp.broadcast_to(rest[p : p + 1], (ROWS, GROUP * BLOCK))
            parts.append(jnp.where(ids == row_of, line, bf16(0)))
        left = jnp.concatenate(parts, axis=0)
        found = lax.dot_general(left, cols[z], (((1,), (1,)), ((), ())), preferred_element_type=f32)
        field[4 * MAIN : (4 + ROWS) * MAIN, :] += found[: ROWS * MAIN]
        tail[...] += found[ROWS * MAIN :]

    def arrive(z, count):
        block = recv.at[pl.ds(z * GROUP, count)]
        pltpu.make_async_copy(block, block, recv_sem.at[z]).wait()

    def place_group(k, carry):
        z = z_of(k)
        arrive(z, GROUP)
        place(z)
        return carry

    lax.fori_loop(0, NZ - 1, place_group, 0)
    own.wait()
    arrive(mz, GROUP - 1)
    place(mz)

    blank = jnp.zeros((8, LON), f32)
    for i, r in enumerate((ROWS - 4, 0)):
        edge_out[i, : 4 * MAIN, :] = field[(4 + r) * MAIN : (8 + r) * MAIN, :].astype(bf16)
        edge_out[i, 4 * MAIN :, :] = jnp.concatenate(
            [tail[r : r + 4, :], tail[ROWS + r : ROWS + r + 4, :], blank], axis=0
        ).astype(bf16)
    edge_copies = []
    for i, other in enumerate((upper, lower)):
        copy = pltpu.make_async_remote_copy(
            src_ref=edge_out.at[i],
            dst_ref=edge_in.at[i],
            send_sem=edge_send.at[i],
            recv_sem=edge_recv.at[i],
            device_id={"lat": other},
            device_id_type=MESH,
        )
        copy.start()
        edge_copies.append(copy)

    for p in range(2):
        for b in range(LON // 128):
            for t in range(2):
                tail_d[pl.ds(32 + t * 64 + b * 2 + p, 8, stride=8), :] = tail[
                    p * ROWS + t * 8 : p * ROWS + t * 8 + 8, b * 128 : (b + 1) * 128
                ]

    def advance(src, first, last, store):
        def line(ref, e):
            return ref[pl.ds(e, 1), :]

        def rows(e):
            return src[pl.ds(pl.multiple_of(e * MAIN, MAIN), MAIN), :]

        def flux_y(e):
            a, b, c, d = main_y
            return (a * rows(e - 1) + b * rows(e) + c * rows(e + 1) + d * rows(e + 2)) * line(open_y, e)

        def step(e, south):
            here = rows(e)
            a, b, c, d = main_x
            east = (
                a * pltpu.roll(here, 1, 1)
                + b * here
                + c * pltpu.roll(here, LON - 1, 1)
                + d * pltpu.roll(here, LON - 2, 1)
            ) * line(open_x, e)
            north = flux_y(e)
            store(e, (here - (east - pltpu.roll(east, 1, 1)) - (north - south)) * line(mask_x, e))
            return north

        lax.fori_loop(first, last, step, flux_y(first - 1))

    def keep(e, new):
        mid[pl.ds(pl.multiple_of(e * MAIN, MAIN), MAIN), :] = new

    def finish(e, new):
        for b in range(LON // 128):
            for h in range(MAIN // 8):
                out_v[b, pl.ds(h * 8 * ROWS + e - 4, 8, stride=ROWS), :] = new[h * 8 : h * 8 + 8, b * 128 : (b + 1) * 128]

    advance(field, 6, 18, keep)
    advance(mid, 8, 16, finish)

    for copy in edge_copies:
        copy.wait()
    for i, (e, there) in enumerate(((0, has_lower), (EXT - 4, has_upper))):
        field[e * MAIN : (e + 4) * MAIN, :] = edge_in[i, : 4 * MAIN, :].astype(f32) * there
        ghost = edge_in[i, 4 * MAIN :, :].astype(f32) * there
        for p in range(2):
            for b in range(LON // 128):
                tail_d[pl.ds(e * 8 + b * 2 + p, 4, stride=8), :] = ghost[p * 4 : p * 4 + 4, b * 128 : (b + 1) * 128]

    advance(field, 2, 6, keep)
    advance(field, 18, 22, keep)
    advance(mid, 4, 8, finish)
    advance(mid, 16, 20, finish)

    lane3 = lax.broadcasted_iota(jnp.int32, (1, 8, 128), 2)

    def west_of(x):
        turned = pltpu.roll(x, 1, 2)
        return jnp.where(lane3 == 0, pltpu.roll(turned, 2, 1), turned)

    def east_of(x, n):
        turned = pltpu.roll(x, 128 - n, 2)
        return jnp.where(lane3 >= 128 - n, pltpu.roll(turned, 6, 1), turned)

    def advance_tail(full, first):
        count = full.shape[0] - 4
        here = full[2 : count + 2]
        shaped = lambda ref, start, n: ref[start * 8 : (start + n) * 8, :].reshape(n, 8, 128)
        a, b, c, d = tail_x
        east = (a * west_of(here) + b * here + c * east_of(here, 1) + d * east_of(here, 2)) * shaped(
            dense_x, first + 2, count
        )
        a, b, c, d = tail_y
        north = (
            a * full[0 : count + 1] + b * full[1 : count + 2] + c * full[2 : count + 3] + d * full[3 : count + 4]
        ) * shaped(dense_y, first + 1, count + 1)
        return (here - (east - west_of(east)) - (north[1:] - north[:-1])) * shaped(dense_m, first + 2, count)

    ext = tail_d[...].reshape(EXT, 8, 128)
    done = advance_tail(advance_tail(ext, 0), 2)
    tail_mid[...] = done.reshape(ROWS * 8, 128)
    for p in range(2):
        for b in range(LON // 128):
            out_v[b, (MAIN + p) * ROWS : (MAIN + p + 1) * ROWS, :] = tail_mid[pl.ds(b * 2 + p, ROWS, stride=8), :]

    outs = [
        pltpu.make_async_copy(out_v.at[b], out_hbm.at[:, pl.ds(b * 128, 128)], out_sem.at[b]) for b in range(LON // 128)
    ]
    for copy in outs:
        copy.start()
    sent = send.at[pl.ds(0, PEERS - 1)]
    pltpu.make_async_copy(sent, sent, send_sem).wait()
    for copy in outs:
        copy.wait()


def body(spectrum, sea_cells, sea_count, refraction, wind_speed, growth, damping, courant):
    vmem, smem, dma = pltpu.VMEM, pltpu.SMEM, pltpu.SemaphoreType.DMA
    table = jnp.asarray(direction_table())
    block = (PEERS, MINE // 2, 2, BLOCK)
    scratch = [
        vmem((NCOMP, BLOCK), bf16),
        vmem((1, SLOTS), jnp.int32),
        smem((1,), jnp.int32),
        vmem((1, BLOCK), f32),
        vmem((1, BLOCK), f32),
        vmem((NCOMP,), f32),
        vmem((NCOMP,), f32),
        smem((32,), f32),
        vmem((2, 24, 128), f32),
        vmem((NCOMP, BLOCK), f32),
        vmem((NCOMP, BLOCK), f32),
        vmem((NCOMP, BLOCK), f32),
        vmem(block, bf16),
        vmem(block, bf16),
        vmem((NZ, LON, GROUP * BLOCK), bf16),
        vmem((NZ, ROWS, GROUP * BLOCK), jnp.int16),
        vmem((ROWS, LON), bf16),
        vmem((2, ROWS, LON), bf16),
        vmem((EXT, LON), f32),
        vmem((EXT, LON), f32),
        vmem((EXT, LON), f32),
        vmem((EXT * 8, 128), f32),
        vmem((EXT * 8, 128), f32),
        vmem((EXT * 8, 128), f32),
        vmem((EXT * MAIN, LON), f32),
        vmem((EXT * MAIN, LON), f32),
        vmem((2 * ROWS, LON), f32),
        vmem((EXT * 8, 128), f32),
        vmem((ROWS * 8, 128), f32),
        vmem((2, 4 * MAIN + 16, LON), bf16),
        vmem((2, 4 * MAIN + 16, LON), bf16),
        vmem((LON // 128, MINE * ROWS, 128), f32),
        dma((9,)),
        dma,
        dma((NZ,)),
        dma,
        dma((2,)),
        dma((2,)),
        dma((2,)),
        dma((2,)),
        dma((LON // 128,)),
    ]
    out = pl.pallas_call(
        kernel,
        out_shape=jax.ShapeDtypeStruct((MINE * ROWS, LON), f32),
        in_specs=[pl.BlockSpec(memory_space=pl.ANY)] * 9,
        out_specs=pl.BlockSpec(memory_space=pl.ANY),
        scratch_shapes=scratch,
        compiler_params=pltpu.CompilerParams(collective_id=0, has_side_effects=True, vmem_limit_bytes=64 << 20),
        name="wave_step",
    )(spectrum, sea_cells, sea_count, refraction, wind_speed, growth, damping, courant, table)
    return out.reshape(MINE, ROWS, LON)


def solution(mesh):
    return jax.shard_map(
        body,
        mesh=mesh,
        in_specs=(
            P(None, ("lat", "comp")),
            P("lat", None),
            P("lat"),
            P("lat", None),
            P("lat", None),
            P(),
            P(),
            P(),
        ),
        out_specs=P("comp", "lat", None),
        check_vma=False,
    )
```

time: 141 us -> 39.3 us (0.28)
  the two profiles are of different devices: /device:TPU:16 before, /device:TPU:1 now
where the time goes in v1:
time: 39.3 us; the launch traced here: 39.1 us
  Pallas kernels  36.5 us (93%)
  local copies, waits for them, and re-layouts  1.93 us (5%)
  between operations  0.66 us (2%)
    pallas_call x1, Pallas kernels, body(): pl.pallas_call(kernel, out_shape=jax.ShapeDtypeStruct((MINE * ROWS, LON),...  36.5 us
    unnamed x1, local copies, waits for them, and re-layouts  1.93 us

profile of v1, /device:TPU:1, one launch (start us, length us, event | category | flops | bytes accessed | tf_op | source)
XLA Modules:
  0.0 39.1 jit_solution(3716746715890058347)
XLA Ops:
  0.7 36.5 %wave_step.1 = f32[288,512]{1,0:T(8,128)} custom-call(bf16[1152,128]{1,0:T(8,128)(2,1)} %spec_hbm.1, s32[1,8192]{1,0:T(1,128)} %cells_hbm.1, s32[1]{0:T(128)S(6)} %copy.11.count_hbm, f32[1,8192]{1,0:T(1,128)} %refr_hbm.1, f32[1,8192]{1,0:T(1,128)} %wind_hbm.1, f32[1152]{0:T(1024)} %growth_hbm.1, f32[1152]{0:T(1024)} %damp_hbm.1, f32[32]{0:T(128)} %cour_hbm.1, ...), custom_call_target="tpu_custom_call" | custom-call | tf_op jit(solution)/shard_map/wave_step/pallas_call | solution.py:422
  37.1 1.9 %copy.12 = f32[18,16,512]{2,1,0:T(8,128)} copy(f32[18,16,512]{2,1,0:T(8,128)} %bitcast.1) | data formatting | bytes 1179648

commit v2 on v1

v2 whole, which is shorter than its diff:
```python
import math

import jax
import jax.numpy as jnp
import numpy as np
from jax import lax
from jax.experimental import pallas as pl
from jax.experimental.pallas import tpu as pltpu
from jax.sharding import PartitionSpec as P

MESH = pl.DeviceIdType.MESH
NDIR = 36
NCOMP = 1152
ROWS = 16
LON = 512
HALF = LON // 2
TILES = 8
SLOTS = 8192
PEERS = 64
NX, NZ, NCORE = 4, 8, 2
GROUP = NX * NCORE
BLOCK = 128
MINE = NCOMP // PEERS
MAIN = 16
EXT = ROWS + 8
CHUNK = 4 * NDIR

f32 = jnp.float32
bf16 = jnp.bfloat16


FIRST_INNER = ((range(6, 14),), (range(10, 18),))
FIRST_OUTER = ((range(2, 6), range(18, 22)),)
SECOND_INNER = ((range(8, 16),),)
SECOND_OUTER = ((range(4, 8), range(16, 20)),)
GROUPS = FIRST_INNER + FIRST_OUTER + SECOND_INNER + SECOND_OUTER


def direction_table():
    angles = np.arange(NDIR, dtype=np.float32) * np.float32(2.0 * math.pi / NDIR)
    pick = list(range(MAIN)) + [MAIN, MAIN + 1] * 4
    table = np.zeros((2, 2, 32, 128), np.float32)
    for half in range(2):
        rows = angles[half * MINE + np.array(pick)]
        across = np.tile(angles[half * MINE : half * MINE + MAIN], 128 // MAIN)
        for i, wave in enumerate((np.cos, np.sin)):
            table[half, i, :24] = wave(rows)[:, None]
            table[half, i, 24:] = wave(across)[None, :]
    return table


def face_weights(speed):
    size = jnp.abs(speed)
    third = (1.0 - speed * speed) / 6.0
    near = (0.5 + 0.5 * size + 2.0 * third) * speed
    far = (0.5 - 0.5 * size - third) * speed
    ahead = speed >= 0.0
    return ahead, -third * speed, jnp.where(ahead, near, far), jnp.where(ahead, far, near)


def kernel(
    spec_hbm, cells_hbm, count_s, refr_hbm, wind_hbm, growth_hbm, damp_hbm, cour_hbm, table_hbm, out,
    spec_v, cells_v, refr_v, wind_v, growth_v, damp_v, cour_s, table_v,
    growth_b, damp_b, bent, send, recv, cols, rowid, mask_bf, mask_in,
    mask_x, open_x, open_y, turned_open, dense_m, dense_x, dense_y,
    field, mid, tail, tail_d, tail_mid, tail_done, edge_out, edge_in, tail_out, tail_in, out_v,
    in_sem, send_sem, recv_sem, own_sem, mask_send, mask_recv, edge_send, edge_recv,
):
    me = lax.axis_index("comp")
    lat = lax.axis_index("lat")
    mx, mz, mc = me // (NZ * NCORE), lax.rem(me, NZ * NCORE) // NCORE, lax.rem(me, NCORE)
    mq = mx * NCORE + mc
    upper, lower = lax.rem(lat + 1, TILES), lax.rem(lat + TILES - 1, TILES)

    barrier = pltpu.get_barrier_semaphore()

    def z_of(k):
        steps = jnp.where(k == 0, NZ // 2, jnp.where(k == 1, 0, NZ // 2 - k // 2))
        return lax.rem(mz + jnp.where(lax.rem(k, 2) == 0, steps, NZ - steps), NZ)

    def device_of(k, j):
        q = lax.rem(mq + j, GROUP)
        return (q // NCORE) * (NZ * NCORE) + z_of(k) * NCORE + lax.rem(q, NCORE)

    def for_peers(act):
        def group(k, carry):
            return lax.fori_loop(jnp.where(k == 1, 1, 0), GROUP, lambda j, c: (act(device_of(k, j)), c)[1], carry)

        lax.fori_loop(0, NZ, group, 0)

    def greet(other):
        pl.semaphore_signal(barrier, inc=1, device_id={"comp": other}, device_id_type=MESH)

    for_peers(greet)
    for other in (upper, lower):
        pl.semaphore_signal(barrier, inc=1, device_id={"lat": other}, device_id_type=MESH)

    my_slots = pl.ds(pl.multiple_of(me * BLOCK, BLOCK), BLOCK)
    loads = [
        (spec_hbm, spec_v),
        (cells_hbm, cells_v),
        (refr_hbm.at[:, my_slots], refr_v),
        (wind_hbm.at[:, my_slots], wind_v),
        (growth_hbm, growth_v),
        (damp_hbm, damp_v),
        (cour_hbm, cour_s),
        (table_hbm.at[lax.rem(me, 2)], table_v),
    ]
    copies = [pltpu.make_async_copy(src, dst, in_sem.at[i]) for i, (src, dst) in enumerate(loads)]
    for copy in copies:
        copy.start()
    for copy in copies:
        copy.wait()

    for j in range(NCOMP // 128):
        part = pl.ds(j * 128, 128)
        growth_b[part, :] = jnp.broadcast_to(growth_v[part].reshape(1, 128), (128, 128)).T
        damp_b[part, :] = jnp.broadcast_to(damp_v[part].reshape(1, 128), (128, 128)).T

    bend = refr_v[...]
    bend_up = jnp.broadcast_to(jnp.maximum(bend, 0.0), (CHUNK, BLOCK))
    bend_down = jnp.broadcast_to(jnp.maximum(-bend, 0.0), (CHUNK, BLOCK))
    dir_of = lax.rem(lax.broadcasted_iota(jnp.int32, (CHUNK, BLOCK), 0), NDIR)

    def refract(g, total):
        part = pl.ds(pl.multiple_of(g * CHUNK, CHUNK), CHUNK)
        energy = spec_v[part, :].astype(f32)
        before = jnp.where(dir_of == 0, pltpu.roll(energy, CHUNK - NDIR + 1, 0), pltpu.roll(energy, 1, 0))
        after = jnp.where(dir_of == NDIR - 1, pltpu.roll(energy, NDIR - 1, 0), pltpu.roll(energy, CHUNK - 1, 0))
        moved = energy + bend_up * (before - energy) + bend_down * (after - energy)
        bent[part, :] = moved
        return total + jnp.sum(moved.reshape(CHUNK // 8, 8, BLOCK), axis=0)

    total = lax.fori_loop(0, NCOMP // CHUNK, refract, jnp.zeros((8, BLOCK), f32))
    mean = jnp.sum(total, axis=0, keepdims=True) / NCOMP
    loss = jnp.broadcast_to(mean / (mean + 1.0), (CHUNK, BLOCK))
    wind = jnp.broadcast_to(wind_v[...], (CHUNK, BLOCK))
    send_rows = send.reshape(NCOMP, BLOCK)

    def source(g, carry):
        part = pl.ds(pl.multiple_of(g * CHUNK, CHUNK), CHUNK)
        rate = growth_b[part, :] * wind - damp_b[part, :] * loss
        send_rows[part, :] = (bent[part, :] * jnp.exp(rate)).astype(bf16)
        return carry

    lax.fori_loop(0, NCOMP // CHUNK, source, 0)

    pl.semaphore_wait(barrier, PEERS - 1 + 2)

    def give(other):
        pltpu.make_async_remote_copy(
            src_ref=send.at[other],
            dst_ref=recv.at[mz * GROUP + mq],
            send_sem=send_sem,
            recv_sem=recv_sem.at[mz],
            device_id={"comp": other},
            device_id_type=MESH,
        ).start()

    for_peers(give)
    own = pltpu.make_async_copy(send.at[me], recv.at[mz * GROUP + mq], own_sem)
    own.start()

    live_count = count_s[0]
    lane = lax.broadcasted_iota(jnp.int32, (1, BLOCK), 1)
    col_of = lax.broadcasted_iota(jnp.int16, (HALF, BLOCK), 0)
    row_of = 2 * lax.broadcasted_iota(jnp.int16, (ROWS, GROUP * BLOCK), 0)

    def factors(z, total):
        for q in range(GROUP):
            first = ((q // NCORE) * (NZ * NCORE) + z * NCORE + q % NCORE) * BLOCK
            cell = cells_v[:, pl.ds(pl.multiple_of(first, BLOCK), BLOCK)]
            col = jnp.broadcast_to(lax.bitwise_and(cell, HALF - 1), (HALF, BLOCK)).astype(jnp.int16)
            cols[z, :, q * BLOCK : (q + 1) * BLOCK] = jnp.where(col_of == col, bf16(1), bf16(0))
            row = jnp.where(lane + first < live_count, lax.shift_right_logical(cell, 8), 2 * ROWS)
            rowid[z, :, q * BLOCK : (q + 1) * BLOCK] = jnp.broadcast_to(row, (ROWS, BLOCK)).astype(jnp.int16)
        ids = rowid[z]
        hot = jnp.concatenate([jnp.where(ids == row_of + half, bf16(1), bf16(0)) for half in range(2)], axis=0)
        return total + lax.dot_general(hot, cols[z], (((1,), (1,)), ((), ())), preferred_element_type=f32)

    mask = lax.fori_loop(0, NZ, factors, jnp.zeros((2 * ROWS, HALF), f32))
    mask = jnp.concatenate([mask[:ROWS], mask[ROWS:]], axis=1)
    mask_bf[...] = mask.astype(bf16)
    mask_copies = []
    for i, other in enumerate((upper, lower)):
        copy = pltpu.make_async_remote_copy(
            src_ref=mask_bf,
            dst_ref=mask_in.at[i],
            send_sem=mask_send.at[i],
            recv_sem=mask_recv.at[i],
            device_id={"lat": other},
            device_id_type=MESH,
        )
        copy.start()
        mask_copies.append(copy)

    field[...] = jnp.zeros_like(field)
    tail[...] = jnp.zeros_like(tail)
    tail_d[...] = jnp.zeros_like(tail_d)
    speed = cour_s[me // 2]
    wx = face_weights(speed * table_v[0])
    wy = face_weights(speed * table_v[1])

    def wide(x, first, count):
        return jnp.concatenate([x[first : first + count]] * (LON // 128), axis=1)

    main_y = [wide(w, 0, MAIN) for w in wy]
    turned_x = [w[24:][None] for w in wx]
    tail_x, tail_y = [[x[MAIN:24][None] for x in w] for w in (wx, wy)]

    for copy in mask_copies:
        copy.wait()
    has_lower = jnp.where(lat > 0, 1.0, 0.0)
    has_upper = jnp.where(lat < TILES - 1, 1.0, 0.0)
    below = mask_in[0].astype(f32)[ROWS - 4 :] * has_lower
    above = mask_in[1].astype(f32)[:4] * has_upper
    full = jnp.concatenate([below, mask, above], axis=0)
    mask_x[...] = full
    open_x[...] = full * pltpu.roll(full, LON - 1, 1)
    open_y[...] = full * pltpu.roll(full, EXT - 1, 0)
    for wide_m, dense in ((mask_x, dense_m), (open_x, dense_x), (open_y, dense_y)):
        for t in range(EXT // 8):
            for b in range(LON // 128):
                piece = wide_m[t * 8 : (t + 1) * 8, b * 128 : (b + 1) * 128]
                for p in range(2):
                    dense[pl.ds(t * 64 + b * 2 + p, 8, stride=8), :] = piece

    for g, runs in enumerate(GROUPS):
        for b in range(LON // 128):
            lines = [
                jnp.broadcast_to(open_x[e : e + 1, b * 128 : (b + 1) * 128], (MAIN, 128)) for run in runs for e in run
            ]
            turned_open[g, b * 128 : (b + 1) * 128, :] = jnp.concatenate(lines, axis=0).T

    recv_rows = recv.reshape(PEERS * MINE, BLOCK)

    edge_rows = (0, 1, 2, 3, ROWS - 4, ROWS - 3, ROWS - 2, ROWS - 1)
    inner_rows = tuple(range(4, ROWS - 4))

    def place(z, rows, with_tail):
        ids = rowid[z]
        starts = [(z * GROUP + q) * MINE for q in range(GROUP)]
        main = jnp.concatenate([recv_rows[pl.ds(first, MAIN), :] for first in starts], axis=1)
        parts = [jnp.where(ids == 2 * r + half, main, bf16(0)) for r in rows for half in range(2)]
        if with_tail:
            rest = jnp.concatenate([recv_rows[pl.ds(first + MAIN, 2), :] for first in starts], axis=1)
            for p in range(2):
                line = jnp.broadcast_to(rest[p : p + 1], (ROWS, GROUP * BLOCK))
                parts += [jnp.where(ids == row_of + half, line, bf16(0)) for half in range(2)]
        left = jnp.concatenate(parts, axis=0)
        found = lax.dot_general(left, cols[z], (((1,), (1,)), ((), ())), preferred_element_type=f32)
        for i, r in enumerate(rows):
            for half in range(2):
                field[4 + r, :, half * HALF : (half + 1) * HALF] += found[(2 * i + half) * MAIN : (2 * i + half + 1) * MAIN]
        if with_tail:
            first = 2 * len(rows) * MAIN
            for half in range(2):
                for p in range(2):
                    start = first + (2 * p + half) * ROWS
                    tail[p * ROWS : (p + 1) * ROWS, half * HALF : (half + 1) * HALF] += found[start : start + ROWS]

    def arrive(z, count):
        block = recv.at[pl.ds(z * GROUP, count)]
        pltpu.make_async_copy(block, block, recv_sem.at[z]).wait()

    def place_both(k, carry):
        place(z_of(k), edge_rows, True)
        place(z_of(k), inner_rows, False)
        return carry

    def place_edges(k, carry):
        arrive(z_of(k), GROUP)
        place(z_of(k), edge_rows, True)
        return carry

    own.wait()
    arrive(mz, GROUP - 1)
    arrive(z_of(0), GROUP)
    lax.fori_loop(0, 2, place_both, 0)
    lax.fori_loop(2, NZ, place_edges, 0)

    forward = lax.rem(me, 2) == 0
    downstream = jnp.where(forward, upper, lower)
    upstream = jnp.where(forward, lower, upper)

    def pack(i, r):
        edge_out[i, :, :] = field[4 + r : 6 + r].reshape(2 * MAIN, LON).astype(bf16)
        pieces = [tail[p * ROWS + r : p * ROWS + r + 2, b * 128 : (b + 1) * 128] for b in range(LON // 128) for p in range(2)]
        tail_out[i, :, :] = jnp.concatenate(pieces, axis=0).astype(bf16)

    pack(0, ROWS - 2)
    pack(1, 0)

    def pack_first(r):
        pieces = [field[e, 0:1, b * 128 : (b + 1) * 128] for b in range(LON // 128) for e in (4 + r, 5 + r)]
        tail_out[3, :, :] = jnp.concatenate(pieces + [jnp.zeros((8, 128), f32)], axis=0).astype(bf16)

    @pl.when(forward)
    def _():
        pack(2, ROWS - 4)
        pack_first(2)

    @pl.when(jnp.logical_not(forward))
    def _():
        pack(2, 2)
        pack_first(ROWS - 4)

    edge_copies = []
    for i, other in enumerate((upper, lower, downstream, upstream)):
        for j, (src, dst) in enumerate(((edge_out, edge_in), (tail_out, tail_in))):
            if i == 3 and j == 0:
                continue
            copy = pltpu.make_async_remote_copy(
                src_ref=src.at[i],
                dst_ref=dst.at[i],
                send_sem=edge_send.at[i, j],
                recv_sem=edge_recv.at[i, j],
                device_id={"lat": other},
                device_id_type=MESH,
            )
            copy.start()
            edge_copies.append(copy)

    lax.fori_loop(2, NZ, lambda k, c: (place(z_of(k), inner_rows, False), c)[1], 0)

    for p in range(2):
        for b in range(LON // 128):
            for t in range(2):
                tail_d[pl.ds(32 + t * 64 + b * 2 + p, 8, stride=8), :] = tail[
                    p * ROWS + t * 8 : p * ROWS + t * 8 + 8, b * 128 : (b + 1) * 128
                ]

    def change_x(src, rows, g):
        blocks = []
        for b in range(LON // 128):
            blocks.append(jnp.concatenate([src[e, :, b * 128 : (b + 1) * 128] for e in rows], axis=0).T)
        now = jnp.concatenate(blocks, axis=0)

        def tiles(x):
            return x.reshape(LON // 8, 8, 128)

        ahead, far, here, there = turned_x
        side = jnp.where(ahead, tiles(pltpu.roll(now, 1, 0)), tiles(pltpu.roll(now, LON - 2, 0)))
        east = far * side + here * tiles(now) + there * tiles(pltpu.roll(now, LON - 1, 0))
        east = (east * tiles(turned_open[g])).reshape(LON, 128)
        change = east - pltpu.roll(east, 1, 0)
        back = [change[b * 128 : (b + 1) * 128].T for b in range(LON // 128)]
        return {e: jnp.concatenate([x[i * MAIN : (i + 1) * MAIN] for x in back], axis=1) for i, e in enumerate(rows)}

    def advance(src, runs, store):
        moved = change_x(src, [e for run in runs for e in run], GROUPS.index(runs))
        ahead, far, here, there = main_y

        def flux_y(e):
            side = jnp.where(ahead, src[e - 1], src[e + 2])
            return (far * side + here * src[e] + there * src[e + 1]) * open_y[e : e + 1, :]

        for run in runs:
            south = flux_y(run[0] - 1)
            for e in run:
                north = flux_y(e)
                store(e, (src[e] - moved[e] - (north - south)) * mask_x[e : e + 1, :])
                south = north

    def keep(e, new):
        mid[e] = new

    def finish(e, new):
        for h in range(MAIN // 8):
            for b in range(LON // 128):
                out_v[b, pl.ds(h * 8 * ROWS + e - 4, 8, stride=ROWS), :] = new[h * 8 : h * 8 + 8, b * 128 : (b + 1) * 128]

    lane3 = lax.broadcasted_iota(jnp.int32, (1, 8, 128), 2)

    def west_of(x):
        turned = pltpu.roll(x, 1, 2)
        return jnp.where(lane3 == 0, pltpu.roll(turned, 2, 1), turned)

    def east_of(x, n):
        turned = pltpu.roll(x, 128 - n, 2)
        return jnp.where(lane3 >= 128 - n, pltpu.roll(turned, 6, 1), turned)

    def rows3(ref, start, count):
        return ref[start * 8 : (start + count) * 8, :].reshape(count, 8, 128)

    def advance_tail(full, first):
        count = full.shape[0] - 4
        now = full[2 : count + 2]
        ahead, far, here, there = tail_x
        side = jnp.where(ahead, west_of(now), east_of(now, 2))
        east = (far * side + here * now + there * east_of(now, 1)) * rows3(dense_x, first + 2, count)
        ahead, far, here, there = tail_y
        side = jnp.where(ahead, full[0 : count + 1], full[3 : count + 4])
        north = (far * side + here * full[1 : count + 2] + there * full[2 : count + 3]) * rows3(
            dense_y, first + 1, count + 1
        )
        return (now - (east - west_of(east)) - (north[1:] - north[:-1])) * rows3(dense_m, first + 2, count)

    for runs in FIRST_INNER:
        advance(field, runs, keep)
    for runs in SECOND_INNER:
        advance(mid, runs, finish)
    tail_half = advance_tail(rows3(tail_d, 4, ROWS), 4)
    tail_mid[48:144, :] = tail_half.reshape(96, 128)
    tail_done[32:96, :] = advance_tail(tail_half, 6).reshape(64, 128)

    for copy in edge_copies:
        copy.wait()
    def unpack(i, e, there):
        field[e : e + 2] = (edge_in[i].astype(f32) * there).reshape(2, MAIN, LON)
        ghost = tail_in[i].astype(f32) * there
        for k in range(8):
            tail_d[pl.ds(e * 8 + k, 2, stride=8), :] = ghost[2 * k : 2 * k + 2]

    unpack(0, 2, has_lower)
    unpack(1, EXT - 4, has_upper)

    def unpack_first(e, there):
        ghost = tail_in[3].astype(f32) * there
        for b in range(LON // 128):
            for i in range(2):
                field[e + i, 0:1, b * 128 : (b + 1) * 128] = ghost[2 * b + i : 2 * b + i + 1]

    @pl.when(forward)
    def _():
        unpack(2, 0, has_lower)
        unpack_first(EXT - 2, has_upper)

    @pl.when(jnp.logical_not(forward))
    def _():
        unpack(2, EXT - 2, has_upper)
        unpack_first(0, has_lower)

    for runs in FIRST_OUTER:
        advance(field, runs, keep)
    for runs in SECOND_OUTER:
        advance(mid, runs, finish)
    low = jnp.concatenate([advance_tail(rows3(tail_d, 0, 8), 0), rows3(tail_mid, 6, 4)], axis=0)
    tail_done[0:32, :] = advance_tail(low, 2).reshape(32, 128)
    high = jnp.concatenate([rows3(tail_mid, 14, 4), advance_tail(rows3(tail_d, 16, 8), 16)], axis=0)
    tail_done[96:128, :] = advance_tail(high, 14).reshape(32, 128)

    for b in range(LON // 128):
        out[: MAIN * ROWS, b * 128 : (b + 1) * 128] = out_v[b]
        for p in range(2):
            out[(MAIN + p) * ROWS : (MAIN + p + 1) * ROWS, b * 128 : (b + 1) * 128] = tail_done[
                pl.ds(b * 2 + p, ROWS, stride=8), :
            ]
    sent = send.at[pl.ds(0, PEERS - 1)]
    pltpu.make_async_copy(sent, sent, send_sem).wait()


def body(spectrum, sea_cells, sea_count, refraction, wind_speed, growth, damping, courant):
    vmem, smem, dma = pltpu.VMEM, pltpu.SMEM, pltpu.SemaphoreType.DMA
    table = jnp.asarray(direction_table())
    block = (PEERS, MINE // 2, 2, BLOCK)
    scratch = [
        vmem((NCOMP, BLOCK), bf16),
        vmem((1, SLOTS), jnp.int32),
        vmem((1, BLOCK), f32),
        vmem((1, BLOCK), f32),
        vmem((NCOMP,), f32),
        vmem((NCOMP,), f32),
        smem((32,), f32),
        vmem((2, 32, 128), f32),
        vmem((NCOMP, BLOCK), f32),
        vmem((NCOMP, BLOCK), f32),
        vmem((NCOMP, BLOCK), f32),
        vmem(block, bf16),
        vmem(block, bf16),
        vmem((NZ, HALF, GROUP * BLOCK), bf16),
        vmem((NZ, ROWS, GROUP * BLOCK), jnp.int16),
        vmem((ROWS, LON), bf16),
        vmem((2, ROWS, LON), bf16),
        vmem((EXT, LON), f32),
        vmem((EXT, LON), f32),
        vmem((EXT, LON), f32),
        vmem((len(GROUPS), LON, 128), f32),
        vmem((EXT * 8, 128), f32),
        vmem((EXT * 8, 128), f32),
        vmem((EXT * 8, 128), f32),
        vmem((EXT, MAIN, LON), f32),
        vmem((EXT, MAIN, LON), f32),
        vmem((2 * ROWS, LON), f32),
        vmem((EXT * 8, 128), f32),
        vmem((EXT * 8, 128), f32),
        vmem((ROWS * 8, 128), f32),
        vmem((3, 2 * MAIN, LON), bf16),
        vmem((3, 2 * MAIN, LON), bf16),
        vmem((4, 16, 128), bf16),
        vmem((4, 16, 128), bf16),
        vmem((LON // 128, MAIN * ROWS, 128), f32),
        dma((8,)),
        dma,
        dma((NZ,)),
        dma,
        dma((2,)),
        dma((2,)),
        dma((4, 2)),
        dma((4, 2)),
    ]
    inputs = (spectrum, sea_cells, sea_count, refraction, wind_speed, growth, damping, courant, table)
    out = pl.pallas_call(
        kernel,
        out_shape=jax.ShapeDtypeStruct((MINE * ROWS, LON), f32),
        in_specs=[pl.BlockSpec(memory_space=pltpu.SMEM if x is sea_count else pltpu.HBM) for x in inputs],
        out_specs=pl.BlockSpec(memory_space=pltpu.VMEM),
        scratch_shapes=scratch,
        compiler_params=pltpu.CompilerParams(collective_id=0, has_side_effects=True, vmem_limit_bytes=40 << 20),
        name="wave_step",
    )(*[x if x is sea_count else pltpu.with_memory_space_constraint(x, pltpu.HBM) for x in inputs])
    return out.reshape(MINE, ROWS, LON)


def solution(mesh):
    return jax.shard_map(
        body,
        mesh=mesh,
        in_specs=(
            P(None, ("lat", "comp")),
            P("lat", None),
            P("lat"),
            P("lat", None),
            P("lat", None),
            P(),
            P(),
            P(),
        ),
        out_specs=P("comp", "lat", None),
        check_vma=False,
    )
```

time: 39.3 us -> 33.4 us (0.85)
  Pallas kernels: 36.5 us -> 31.7 us
  local copies, waits for them, and re-layouts: 1.93 us -> 0.82 us
    pallas_call x1, Pallas kernels: 36.5 us -> 31.7 us  [body(): pl.pallas_call(kernel, out_shape=jax.ShapeDtypeStruct((MINE * ROWS, LON),...]
    unnamed x1, local copies, waits for them, and re-layouts: 1.93 us -> 0.82 us
where the time goes in v2:
time: 33.4 us; the launch traced here: 33.2 us
  Pallas kernels  31.7 us (95%)
  local copies, waits for them, and re-layouts  0.82 us (2%)
  between operations  0.66 us (2%)
    pallas_call x1, Pallas kernels, body(): pl.pallas_call(kernel, out_shape=jax.ShapeDtypeStruct((MINE * ROWS, LON),...  31.7 us
    unnamed x1, local copies, waits for them, and re-layouts  0.82 us

profile of v2, /device:TPU:1, one launch (start us, length us, event | category | flops | bytes accessed | tf_op | source)
XLA Modules:
  0.0 33.2 jit_solution(17970037625346998788)
XLA Ops:
  0.7 31.7 %wave_step.1 = f32[288,512]{1,0:T(8,128)S(1)} custom-call(bf16[1152,128]{1,0:T(8,128)(2,1)} %spec_hbm.1, s32[1,8192]{1,0:T(1,128)} %cells_hbm.1, s32[1]{0:T(128)S(6)} %copy.11.count_s, f32[1,8192]{1,0:T(1,128)} %refr_hbm.1, f32[1,8192]{1,0:T(1,128)} %wind_hbm.1, f32[1152]{0:T(1024)} %growth_hbm.1, f32[1152]{0:T(1024)} %damp_hbm.1, f32[32]{0:T(128)} %cour_hbm.1, ...), custom_call_target="tpu_custom_call" | custom-call | tf_op jit(solution)/shard_map/wave_step/pallas_call | solution.py:503
  32.4 0.8 %copy.12 = f32[18,16,512]{2,1,0:T(8,128)} copy(f32[18,16,512]{2,1,0:T(8,128)S(1)} %bitcast.1) | data formatting | bytes 1179648

commit v3 on v2

--- a/solution.py
+++ b/solution.py
@@ -14,6 +14,7 @@
 ROWS = 16
 LON = 512
 HALF = LON // 2
+BATCH = 2
 TILES = 8
 SLOTS = 8192
 PEERS = 64
@@ -68,23 +69,23 @@
 ):
     me = lax.axis_index("comp")
     lat = lax.axis_index("lat")
-    mx, mz, mc = me // (NZ * NCORE), lax.rem(me, NZ * NCORE) // NCORE, lax.rem(me, NCORE)
+    mx, mz, mc = lax.div(me, NZ * NCORE), lax.div(lax.rem(me, NZ * NCORE), NCORE), lax.rem(me, NCORE)
     mq = mx * NCORE + mc
     upper, lower = lax.rem(lat + 1, TILES), lax.rem(lat + TILES - 1, TILES)
 
     barrier = pltpu.get_barrier_semaphore()
 
-    def z_of(k):
-        steps = jnp.where(k == 0, NZ // 2, jnp.where(k == 1, 0, NZ // 2 - k // 2))
-        return lax.rem(mz + jnp.where(lax.rem(k, 2) == 0, steps, NZ - steps), NZ)
-
-    def device_of(k, j):
-        q = lax.rem(mq + j, GROUP)
-        return (q // NCORE) * (NZ * NCORE) + z_of(k) * NCORE + lax.rem(q, NCORE)
-
     def for_peers(act):
-        def group(k, carry):
-            return lax.fori_loop(jnp.where(k == 1, 1, 0), GROUP, lambda j, c: (act(device_of(k, j)), c)[1], carry)
+        def group(z, carry):
+            q = mq
+            for j in range(GROUP):
+                other = lax.div(q, NCORE) * (NZ * NCORE) + lax.rem(q, NCORE) + z * NCORE
+                if j == 0:
+                    pl.when(z != mz)(lambda other=other: act(other))
+                else:
+                    act(other)
+                q = jnp.where(q == GROUP - 1, 0, q + 1)
+            return carry
 
         lax.fori_loop(0, NZ, group, 0)
 
@@ -237,7 +238,7 @@
     edge_rows = (0, 1, 2, 3, ROWS - 4, ROWS - 3, ROWS - 2, ROWS - 1)
     inner_rows = tuple(range(4, ROWS - 4))
 
-    def place(z, rows, with_tail):
+    def left_factor(z, rows, with_tail):
         ids = rowid[z]
         starts = [(z * GROUP + q) * MINE for q in range(GROUP)]
         main = jnp.concatenate([recv_rows[pl.ds(first, MAIN), :] for first in starts], axis=1)
@@ -247,8 +248,12 @@
             for p in range(2):
                 line = jnp.broadcast_to(rest[p : p + 1], (ROWS, GROUP * BLOCK))
                 parts += [jnp.where(ids == row_of + half, line, bf16(0)) for half in range(2)]
-        left = jnp.concatenate(parts, axis=0)
-        found = lax.dot_general(left, cols[z], (((1,), (1,)), ((), ())), preferred_element_type=f32)
+        return jnp.concatenate(parts, axis=0)
+
+    def place(zs, rows, with_tail):
+        left = jnp.concatenate([left_factor(z, rows, with_tail) for z in zs], axis=1)
+        right = jnp.concatenate([cols[z] for z in zs], axis=1)
+        found = lax.dot_general(left, right, (((1,), (1,)), ((), ())), preferred_element_type=f32)
         for i, r in enumerate(rows):
             for half in range(2):
                 field[4 + r, :, half * HALF : (half + 1) * HALF] += found[(2 * i + half) * MAIN : (2 * i + half + 1) * MAIN]
@@ -263,21 +268,29 @@
         block = recv.at[pl.ds(z * GROUP, count)]
         pltpu.make_async_copy(block, block, recv_sem.at[z]).wait()
 
-    def place_both(k, carry):
-        place(z_of(k), edge_rows, True)
-        place(z_of(k), inner_rows, False)
+    def z_of(k):
+        steps = lax.div(k + 1, 2)
+        return lax.rem(mz + jnp.where(lax.rem(k, 2) == 1, steps, NZ - steps), NZ)
+
+    def place_edges(i, carry):
+        zs = [z_of(i * BATCH + k) for k in range(BATCH)]
+
+        @pl.when(i > 0)
+        def _():
+            arrive(zs[0], GROUP)
+
+        for z in zs[1:]:
+            arrive(z, GROUP)
+        place(zs, edge_rows, True)
         return carry
 
-    def place_edges(k, carry):
-        arrive(z_of(k), GROUP)
-        place(z_of(k), edge_rows, True)
+    def place_inner(i, carry):
+        place([i * BATCH + k for k in range(BATCH)], inner_rows, False)
         return carry
 
     own.wait()
     arrive(mz, GROUP - 1)
-    arrive(z_of(0), GROUP)
-    lax.fori_loop(0, 2, place_both, 0)
-    lax.fori_loop(2, NZ, place_edges, 0)
+    lax.fori_loop(0, NZ // BATCH, place_edges, 0)
 
     forward = lax.rem(me, 2) == 0
     downstream = jnp.where(forward, upper, lower)
@@ -321,7 +334,7 @@
             copy.start()
             edge_copies.append(copy)
 
-    lax.fori_loop(2, NZ, lambda k, c: (place(z_of(k), inner_rows, False), c)[1], 0)
+    lax.fori_loop(0, NZ // BATCH, place_inner, 0)
 
     for p in range(2):
         for b in range(LON // 128):

time: 33.4 us -> 30.2 us (0.904)
  Pallas kernels: 31.7 us -> 28.6 us
    pallas_call x1, Pallas kernels: 31.7 us -> 28.6 us  [body(): pl.pallas_call(kernel, out_shape=jax.ShapeDtypeStruct((MINE * ROWS, LON),...]
where the time goes in v3:
time: 30.2 us; the launch traced here: 30.1 us
  Pallas kernels  28.6 us (95%)
  local copies, waits for them, and re-layouts  0.82 us (3%)
  between operations  0.66 us (2%)
    pallas_call x1, Pallas kernels, body(): pl.pallas_call(kernel, out_shape=jax.ShapeDtypeStruct((MINE * ROWS, LON),...  28.6 us
    unnamed x1, local copies, waits for them, and re-layouts  0.82 us

profile of v3, /device:TPU:1, one launch (start us, length us, event | category | flops | bytes accessed | tf_op | source)
XLA Modules:
  0.0 30.1 jit_solution(18024888415209633948)
XLA Ops:
  0.7 28.6 %wave_step.1 = f32[288,512]{1,0:T(8,128)S(1)} custom-call(bf16[1152,128]{1,0:T(8,128)(2,1)} %spec_hbm.1, s32[1,8192]{1,0:T(1,128)} %cells_hbm.1, s32[1]{0:T(128)S(6)} %copy.11.count_s, f32[1,8192]{1,0:T(1,128)} %refr_hbm.1, f32[1,8192]{1,0:T(1,128)} %wind_hbm.1, f32[1152]{0:T(1024)} %growth_hbm.1, f32[1152]{0:T(1024)} %damp_hbm.1, f32[32]{0:T(128)} %cour_hbm.1, ...), custom_call_target="tpu_custom_call" | custom-call | tf_op jit(solution)/shard_map/wave_step/pallas_call | solution.py:516
  29.3 0.8 %copy.12 = f32[18,16,512]{2,1,0:T(8,128)} copy(f32[18,16,512]{2,1,0:T(8,128)S(1)} %bitcast.1) | data formatting | bytes 1179648

commit v4 on v3

--- a/solution.py
+++ b/solution.py
@@ -60,8 +60,8 @@
 
 
 def kernel(
-    spec_hbm, cells_hbm, count_s, refr_hbm, wind_hbm, growth_hbm, damp_hbm, cour_hbm, table_hbm, out,
-    spec_v, cells_v, refr_v, wind_v, growth_v, damp_v, cour_s, table_v,
+    spec_hbm, cells_hbm, count_hbm, refr_hbm, wind_hbm, growth_hbm, damp_hbm, cour_hbm, table_hbm, out,
+    spec_v, cells_v, count_v, refr_v, wind_v, growth_v, damp_v, cour_s, table_v,
     growth_b, damp_b, bent, send, recv, cols, rowid, mask_bf, mask_in,
     mask_x, open_x, open_y, turned_open, dense_m, dense_x, dense_y,
     field, mid, tail, tail_d, tail_mid, tail_done, edge_out, edge_in, tail_out, tail_in, out_v,
@@ -100,6 +100,7 @@
     loads = [
         (spec_hbm, spec_v),
         (cells_hbm, cells_v),
+        (count_hbm, count_v),
         (refr_hbm.at[:, my_slots], refr_v),
         (wind_hbm.at[:, my_slots], wind_v),
         (growth_hbm, growth_v),
@@ -162,7 +163,7 @@
     own = pltpu.make_async_copy(send.at[me], recv.at[mz * GROUP + mq], own_sem)
     own.start()
 
-    live_count = count_s[0]
+    live_count = count_v[...]
     lane = lax.broadcasted_iota(jnp.int32, (1, BLOCK), 1)
     col_of = lax.broadcasted_iota(jnp.int16, (HALF, BLOCK), 0)
     row_of = 2 * lax.broadcasted_iota(jnp.int16, (ROWS, GROUP * BLOCK), 0)
@@ -269,18 +270,13 @@
         pltpu.make_async_copy(block, block, recv_sem.at[z]).wait()
 
     def z_of(k):
-        steps = lax.div(k + 1, 2)
-        return lax.rem(mz + jnp.where(lax.rem(k, 2) == 1, steps, NZ - steps), NZ)
+        return jnp.where(k < NZ // 2, k, NZ + NZ // 2 - 1 - k)
 
     def place_edges(i, carry):
         zs = [z_of(i * BATCH + k) for k in range(BATCH)]
 
-        @pl.when(i > 0)
-        def _():
-            arrive(zs[0], GROUP)
-
-        for z in zs[1:]:
-            arrive(z, GROUP)
+        for z in zs:
+            pl.when(z != mz)(lambda z=z: arrive(z, GROUP))
         place(zs, edge_rows, True)
         return carry
 
@@ -296,30 +292,21 @@
     downstream = jnp.where(forward, upper, lower)
     upstream = jnp.where(forward, lower, upper)
 
-    def pack(i, r):
-        edge_out[i, :, :] = field[4 + r : 6 + r].reshape(2 * MAIN, LON).astype(bf16)
-        pieces = [tail[p * ROWS + r : p * ROWS + r + 2, b * 128 : (b + 1) * 128] for b in range(LON // 128) for p in range(2)]
+    def tail_rows(p, r, b):
+        return tail[p * ROWS + r : p * ROWS + r + 2, b * 128 : (b + 1) * 128]
+
+    def pack(i, r, r_back):
+        edge_out[i, :, :] = field[pl.ds(4 + (r if r == r_back else jnp.where(forward, r, r_back)), 2)].reshape(2 * MAIN, LON).astype(bf16)
+        pieces = [jnp.where(forward, tail_rows(p, r, b), tail_rows(p, r_back, b)) for b in range(LON // 128) for p in range(2)]
         tail_out[i, :, :] = jnp.concatenate(pieces, axis=0).astype(bf16)
-
-    pack(0, ROWS - 2)
-    pack(1, 0)
 
     def pack_first(r):
         pieces = [field[e, 0:1, b * 128 : (b + 1) * 128] for b in range(LON // 128) for e in (4 + r, 5 + r)]
         tail_out[3, :, :] = jnp.concatenate(pieces + [jnp.zeros((8, 128), f32)], axis=0).astype(bf16)
 
-    @pl.when(forward)
-    def _():
-        pack(2, ROWS - 4)
-        pack_first(2)
-
-    @pl.when(jnp.logical_not(forward))
-    def _():
-        pack(2, 2)
-        pack_first(ROWS - 4)
-
     edge_copies = []
-    for i, other in enumerate((upper, lower, downstream, upstream)):
+
+    def swap(i, other):
         for j, (src, dst) in enumerate(((edge_out, edge_in), (tail_out, tail_in))):
             if i == 3 and j == 0:
                 continue
@@ -334,6 +321,15 @@
             copy.start()
             edge_copies.append(copy)
 
+    pack(2, ROWS - 4, 2)
+    swap(2, downstream)
+    pack(0, ROWS - 2, ROWS - 2)
+    swap(0, upper)
+    pack(1, 0, 0)
+    swap(1, lower)
+    pack_first(jnp.where(forward, 2, ROWS - 4))
+    swap(3, upstream)
+
     lax.fori_loop(0, NZ // BATCH, place_inner, 0)
 
     for p in range(2):
@@ -470,6 +466,7 @@
     scratch = [
         vmem((NCOMP, BLOCK), bf16),
         vmem((1, SLOTS), jnp.int32),
+        vmem((1, BLOCK), jnp.int32),
         vmem((1, BLOCK), f32),
         vmem((1, BLOCK), f32),
         vmem((NCOMP,), f32),
@@ -503,7 +500,7 @@
         vmem((4, 16, 128), bf16),
         vmem((4, 16, 128), bf16),
         vmem((LON // 128, MAIN * ROWS, 128), f32),
-        dma((8,)),
+        dma((9,)),
         dma,
         dma((NZ,)),
         dma,
@@ -512,16 +509,17 @@
         dma((4, 2)),
         dma((4, 2)),
     ]
-    inputs = (spectrum, sea_cells, sea_count, refraction, wind_speed, growth, damping, courant, table)
+    counts = jnp.broadcast_to(sea_count[None, :], (1, BLOCK))
+    inputs = (spectrum, sea_cells, counts, refraction, wind_speed, growth, damping, courant, table)
     out = pl.pallas_call(
         kernel,
         out_shape=jax.ShapeDtypeStruct((MINE * ROWS, LON), f32),
-        in_specs=[pl.BlockSpec(memory_space=pltpu.SMEM if x is sea_count else pltpu.HBM) for x in inputs],
+        in_specs=[pl.BlockSpec(memory_space=pltpu.HBM)] * len(inputs),
         out_specs=pl.BlockSpec(memory_space=pltpu.VMEM),
         scratch_shapes=scratch,
         compiler_params=pltpu.CompilerParams(collective_id=0, has_side_effects=True, vmem_limit_bytes=40 << 20),
         name="wave_step",
-    )(*[x if x is sea_count else pltpu.with_memory_space_constraint(x, pltpu.HBM) for x in inputs])
+    )(*[pltpu.with_memory_space_constraint(x, pltpu.HBM) for x in inputs])
     return out.reshape(MINE, ROWS, LON)
 
 

time: 30.2 us -> 30.9 us (1.023)
  local copies, waits for them, and re-layouts: 0.82 us -> 1.41 us
    broadcast_in_dim x0 -> x1, local copies, waits for them, and re-layouts: none -> 0.59 us  [body(): counts = jnp.broadcast_to(sea_count[None, :], (1, BLOCK))]
where the time goes in v4:
time: 30.9 us; the launch traced here: 30.8 us
  Pallas kernels  28.7 us (93%)
  local copies, waits for them, and re-layouts  1.41 us (5%)
  between operations  0.66 us (2%)
    pallas_call x1, Pallas kernels, body(): pl.pallas_call(kernel, out_shape=jax.ShapeDtypeStruct((MINE * ROWS, LON),...  28.7 us
    unnamed x1, local copies, waits for them, and re-layouts  0.82 us

profile of v4, /device:TPU:1, one launch (start us, length us, event | category | flops | bytes accessed | tf_op | source)
XLA Modules:
  0.0 30.8 jit_solution(1479465488068407001)
XLA Ops:
  0.7 0.6 %broadcast_in_dim.9.count_hbm = s32[1,128]{1,0:T(1,128)} broadcast(s32[]{:T(128)} %bitcast.2), dimensions={} | broadcast | bytes 516 | tf_op jit(solution)/shard_map/broadcast_in_dim | solution.py:512
  1.2 28.7 %wave_step.1 = f32[288,512]{1,0:T(8,128)S(1)} custom-call(bf16[1152,128]{1,0:T(8,128)(2,1)} %spec_hbm.1, s32[1,8192]{1,0:T(1,128)} %cells_hbm.1, s32[1,128]{1,0:T(1,128)} %broadcast_in_dim.9.count_hbm, f32[1,8192]{1,0:T(1,128)} %refr_hbm.1, f32[1,8192]{1,0:T(1,128)} %wind_hbm.1, f32[1152]{0:T(1024)} %growth_hbm.1, f32[1152]{0:T(1024)} %damp_hbm.1, ...), custom_call_target="tpu_custom_call" | custom-call | tf_op jit(solution)/shard_map/wave_step/pallas_call | solution.py:514
  29.9 0.8 %copy.12 = f32[18,16,512]{2,1,0:T(8,128)} copy(f32[18,16,512]{2,1,0:T(8,128)S(1)} %bitcast.3) | data formatting | bytes 1179648
